TPU v7x, 256 devices: a whole 4x4x8 slice. The times are simulated.
256 devices in a mesh: ctx: 32 (over y, z), tp: 8 (over x, core).
Axes of the slice: x: 4, y: 4, z: 8, core: 2. Of those that a mesh axis runs over, the one named last changes fastest.
Arguments:
- hidden: bfloat16 [512, 8192], P('ctx')
- weight: bfloat16 [8192, 98304], P(None, ('ctx', 'tp'))
- targets: int32 [512], replicated, may hold values from 0 to 98303
- row_seq: int32 [512], replicated, may hold values from 0 to 1, as said below
- ref_logp: float32 [2], replicated, may hold values from -120 to 120
Outputs:
- dpo_loss: float32 [], replicated
- d_hidden: bfloat16 [512, 8192], P('ctx', 'tp')
- d_weight: bfloat16 [8192, 98304], P(None, ('ctx', 'tp'))
Inputs may be any that keep to these rules, and one draw needn't show every extreme that they name: `row_seq`: each of 0 and 1 names exactly 256 rows.
All inputs are finite; a program needn't handle non-finite values.
Results may differ from a plain program's by a relative error of at most 0.023.
Values may be sent and summed in bfloat16 or wider, within the bound.
A program may use at most 128 MiB of HBM per device.

v0:
```python
import jax
import jax.numpy as jnp
from jax import lax
from jax.sharding import PartitionSpec as P

SEQS = 2


DPO_BETA = 0.01
LOSS_SCALE = 1024.0


def on_device(hidden, weight, targets, row_seq, ref_logp):
    all_rows = lax.all_gather(hidden, "ctx", axis=0, tiled=True)
    logits = jnp.dot(all_rows, weight, preferred_element_type=jnp.float32)
    vocab_width = weight.shape[1]
    first_column = lax.axis_index(("ctx", "tp")) * vocab_width
    columns = first_column + lax.iota(jnp.int32, vocab_width)
    matches = columns[None, :] == targets[:, None]
    picked = jnp.sum(jnp.where(matches, logits, jnp.float32(0.0)), axis=1)
    local_peak = jnp.max(logits, axis=1)
    row_peak = lax.pmax(local_peak, ("ctx", "tp"))
    local_total = jnp.sum(jnp.exp(logits - row_peak[:, None]), axis=1)
    row_total, target_logit = lax.psum((local_total, picked), ("ctx", "tp"))
    lse = row_peak + jnp.log(row_total)
    row_logp = target_logit - lse
    member = (row_seq[:, None] == jnp.arange(SEQS, dtype=jnp.int32)[None, :]).astype(jnp.float32)
    seq_logp = jnp.sum(member * row_logp[:, None], axis=0)
    margin = DPO_BETA * (seq_logp[0] - ref_logp[0] - (seq_logp[1] - ref_logp[1]))
    dpo_loss = jax.nn.softplus(-margin)
    pull_scale = LOSS_SCALE * DPO_BETA * jax.nn.sigmoid(-margin)
    seq_coef = jnp.stack([-pull_scale, pull_scale])
    row_coef = jnp.sum(member * seq_coef[None, :], axis=1)
    softmax_rows = jnp.exp(logits - lse[:, None])
    grad_logits = (row_coef[:, None] * (matches.astype(jnp.float32) - softmax_rows)).astype(
        jnp.bfloat16
    )
    d_weight = lax.dot_general(
        all_rows, grad_logits, (((0,), (0,)), ((), ())), preferred_element_type=jnp.float32
    ).astype(jnp.bfloat16)
    partial_sums = lax.dot_general(
        grad_logits, weight, (((1,), (1,)), ((), ())), preferred_element_type=jnp.float32
    )
    narrow = lax.psum_scatter(
        partial_sums.astype(jnp.bfloat16), "tp", scatter_dimension=1, tiled=True
    )
    d_hidden = lax.psum_scatter(narrow, "ctx", scatter_dimension=0, tiled=True)
    return (dpo_loss, d_hidden, d_weight)


def solution(mesh):
    placed = (P("ctx", None), P(None, ("ctx", "tp")), P(), P(), P())
    return jax.shard_map(
        on_device,
        mesh=mesh,
        in_specs=placed,
        out_specs=(P(), P("ctx", "tp"), P(None, ("ctx", "tp"))),
        check_vma=False,
    )
```

profile of v0, /device:TPU:6, one launch (start us, length us, event | category | flops | bytes accessed | tf_op | source)
XLA Modules:
  0.0 560.2 jit_solution(8189828101533610389)
XLA Ops:
  7.2 0.0 all-gather.2.cloned.1.call-start
  7.2 0.7 all-gather.2.cloned.1.call-update
  7.9 0.0 reduce-scatter.3.cloned.1.call-start
  8.0 0.0 copy-start.1
  8.0 0.0 copy-start
  8.0 0.0 copy-start.2
  8.0 104.1 %all-gather.2.cloned.1.call-done = bf16[512,8192]{1,0:T(8,128)(2,1)} async-done(((bf16[16,8192]{1,0:T(8,128)(2,1)}), bf16[512,8192]{1,0:T(8,128)(2,1)}) %all-gather.2.cloned.1.call-update) | async-done | bytes 8388624 | tf_op jit(solution)/shard_map/all_gather | solution.py:14
  112.1 8.9 %fusion.10 = (f32[512]{0:T(512)S(1)}, f32[512,384]{0,1:T(8,128)S(1)}) fusion(bf16[512,8192]{1,0:T(8,128)(2,1)} %all-gather.2.cloned.1.call-done, bf16[8192,384]{1,0:T(8,128)(2,1)} %param.6), kind=kOutput, calls=%fused_computation.19 | convolution fusion | flops 3221421568 | bytes 15468544 | tf_op jit(solution)/shard_map/dot_general | solution.py:15
  120.9 73.9 %pmax.7 = f32[512]{0:T(512)S(1)} all-reduce(f32[512]{0:T(512)S(1)} %get-tuple-element.19), channel_id=1, replica_groups=mesh['ctx'=32,'tp'=8] {'ctx','tp'}, use_global_device_ids=true, to_apply=%region_3.4 | all-reduce | flops 512 | bytes 4096 | tf_op jit(solution)/shard_map/pmax | solution.py:22
  194.8 0.0 copy-done.1
  194.8 0.2 exponential_reduce_fusion
  195.0 73.3 %all-reduce = (f32[512]{0:T(512)S(1)}, f32[512]{0:T(512)S(1)}) all-reduce(f32[512]{0:T(512)S(1)} %get-tuple-element.10, f32[512]{0:T(512)S(1)} %get-tuple-element.9), channel_id=1, replica_groups=mesh['ctx'=32,'tp'=8] {'ctx','tp'}, use_global_device_ids=true, to_apply=%region_1.2 | all-reduce | flops 1024 | bytes 8192 | tf_op jit(solution)/shard_map/psum | solution.py:24
  268.4 0.0 copy-done
  268.4 0.1 select_reduce_fusion.1
  268.5 0.0 copy-done.2
  268.5 0.6 fusion.8
  271.7 0.1 pad_maximum_fusion
  271.8 0.1 select_reduce_fusion
  271.8 9.7 %convolution_convert_fusion = bf16[512,8192]{1,0:T(8,128)(2,1)} fusion(bf16[8192,384]{1,0:T(8,128)(2,1)} %param.6, f32[512,384]{0,1:T(8,128)S(1)} %get-tuple-element.20, f32[512]{0:T(512)S(1)} %get-tuple-element.14, f32[512]{0:T(512)S(1)} %select_reduce_fusion, s32[512]{0:T(512)S(1)} %copy-done.1, s32[384]{0:T(512)S(1)} %iota_add_fusion), kind=kOutput, calls=%fused_computation | convolution fusion | flops 3226599424 | bytes 15474176 | tf_op jit(solution)/shard_map/dot_general | solution.py:41
  281.6 0.0 reduce-scatter.3.cloned.1.call-update
  281.6 0.0 reduce-scatter.5.cloned.1.call-start
  281.7 50.5 %reduce-scatter.3.cloned.1.call-done = bf16[512,1024]{1,0:T(8,128)(2,1)} async-done(((bf16[512,8192]{1,0:T(8,128)(2,1)}), bf16[512,1024]{1,0:T(8,128)(2,1)}) %reduce-scatter.3.cloned.1.call-update) | async-done | bytes 1048592 | tf_op jit(solution)/shard_map/reduce_scatter | solution.py:44
  332.2 0.0 reduce-scatter.5.cloned.1.call-update
  332.3 9.0 %fusion = bf16[8192,384]{0,1:T(8,128)(2,1)} fusion(bf16[512,8192]{1,0:T(8,128)(2,1)} %all-gather.2.cloned.1.call-done, f32[512,384]{0,1:T(8,128)S(1)} %get-tuple-element.20, f32[512]{0:T(512)S(1)} %get-tuple-element.14, f32[512]{0:T(512)S(1)} %select_reduce_fusion, s32[512]{0:T(512)S(1)} %copy-done.1, s32[384]{0:T(512)S(1)} %iota_add_fusion), kind=kOutput, calls=%fused_computation.2 | convolution fusion | flops 3225550848 | bytes 15474176 | tf_op jit(solution)/shard_map/dot_general | solution.py:38
  341.3 8.6 %copy.9 = bf16[8192,384]{1,0:T(8,128)(2,1)} copy(bf16[8192,384]{0,1:T(8,128)(2,1)} %fusion) | data formatting | bytes 12582912
  349.9 202.6 %reduce-scatter.5.cloned.1.call-done = bf16[16,1024]{1,0:T(8,128)(2,1)} async-done(((bf16[512,1024]{1,0:T(8,128)(2,1)}), bf16[16,1024]{1,0:T(8,128)(2,1)}) %reduce-scatter.5.cloned.1.call-update) | async-done | bytes 32784 | tf_op jit(solution)/shard_map/reduce_scatter | solution.py:47
  (2 shorter events, 0.0 us)
Async XLA Ops:
  7.2 104.9 %all-gather.2.cloned.1.call-start = ((), (), s32[]{:S(2)}) async-start(), calls=%async_computation.2 | async-start | bytes 8650752 | tf_op jit(solution)/shard_map/all_gather | solution.py:14
  7.9 324.3 %reduce-scatter.3.cloned.1.call-start = ((), (), s32[]{:S(2)}) async-start(), calls=%async_computation.3 | async-start | bytes 9437184 | tf_op jit(solution)/shard_map/reduce_scatter | solution.py:44
  8.0 186.8 %copy-start.1 = (s32[512]{0:T(512)S(1)}, s32[512]{0:T(512)}, u32[]{:S(2)}) copy-start(s32[512]{0:T(512)} %param.7) | copy-start | bytes 6148
  8.0 260.4 %copy-start = (s32[512]{0:T(512)S(1)}, s32[512]{0:T(512)}, u32[]{:S(2)}) copy-start(s32[512]{0:T(512)} %param.8) | copy-start | bytes 6148
  8.0 260.5 %copy-start.2 = (f32[2]{0:T(128)S(1)}, f32[2]{0:T(128)}, u32[]{:S(2)}) copy-start(f32[2]{0:T(128)} %param.9) | copy-start | bytes 28
  281.6 270.9 %reduce-scatter.5.cloned.1.call-start = ((), (), s32[]{:S(2)}) async-start(), calls=%async_computation.4 | async-start | bytes 1081344 | tf_op jit(solution)/shard_map/reduce_scatter | solution.py:47
Sparse Core Ops, SparseCore 0:
  10.6 101.4 all-gather.1
  281.7 50.4 reduce-scatter.2
  336.6 215.8 reduce-scatter.4
where the time goes:
time: 561 us; the launch traced here: 560 us
  waiting for transfers between devices  358 us (64%)
  blocking collectives  147 us (26%)
  matrix products  27.6 us (5%)
  between operations  17.6 us (3%)
  local copies, waits for them, and re-layouts  9.22 us (2%)
    reduce_scatter x1, waiting for transfers between devices, on_device(): d_hidden = lax.psum_scatter(narrow, 'ctx', scatter_dimension=0, tiled=True)  203 us
    all_gather x1, waiting for transfers between devices, on_device(): all_rows = lax.all_gather(hidden, 'ctx', axis=0, tiled=True)  104 us
    pmax x1, blocking collectives, on_device(): row_peak = lax.pmax(local_peak, ('ctx', 'tp'))  73.9 us
    psum x1, blocking collectives, on_device(): row_total, target_logit = lax.psum((local_total, picked), ('ctx', 'tp'))  73.3 us
    reduce_scatter x1, waiting for transfers between devices, on_device(): lax.psum_scatter(partial_sums.astype(jnp.bfloat16), 'tp', scatter_dimensi...  50.5 us
  transfers between devices with their start and end apart: 3, of which 3 were waited for; matrix products, arithmetic and copies ran while one was open for 3% of the time, Pallas kernels for 0%

commit v1 on v0

v1 whole, which is shorter than its diff:
```python
import functools

import jax
import jax.numpy as jnp
from jax import lax
from jax.experimental import pallas as pl
from jax.experimental.pallas import tpu as pltpu
from jax.sharding import PartitionSpec as P

MESH = pl.DeviceIdType.MESH
F32 = jnp.float32
BF16 = jnp.bfloat16

DPO_BETA = 0.01
LOSS_SCALE = 1024.0

NX, NY, NZ = 4, 4, 8
ROWS = 512
D = 8192
VSH = 384
HALF = 4096

GA, GB, GQ = 1024, 1536, 384
SX, SY, SZ = 384, 384, 256

N_SEM = 200


def fused_kernel(
    hid_ref, w_ref, tgt_ref, seq_ref, ref_ref,
    all_ref, grad_ref, loss_ref, dh_ref,
    H, W, logits_t, G,
    st_own, st_core, st_xy, st_z,
    psx, psy, psz, plx, ply, plz, sx, sy, sz,
    lx1, lx2, lx3, ly1, ly2, ly3, lz1h, lz1, lz2, lz3,
    rx2, ry2,
    local_sem, ssem, rsem,
):
    ctx = lax.axis_index("ctx")
    tp = lax.axis_index("tp")
    y = ctx // NZ
    z = lax.rem(ctx, NZ)
    x = tp // 2
    c = lax.rem(tp, 2)

    def wrap(v, n):
        return lax.rem(v + n, n)

    def dev(dy=0, dz=0, dx=0, dc=0):
        yy = wrap(y + dy, NY) if dy else y
        zz = wrap(z + dz, NZ) if dz else z
        xx = wrap(x + dx, NX) if dx else x
        cc = 1 - c if dc else c
        return (yy * NZ + zz, xx * 2 + cc)

    counter = [0]
    sends = []

    def remote(src, dst, **d):
        i = counter[0]
        counter[0] += 1
        copy = pltpu.make_async_remote_copy(
            src_ref=src, dst_ref=dst, send_sem=ssem.at[i], recv_sem=rsem.at[i],
            device_id=dev(**d), device_id_type=MESH,
        )
        copy.start()
        sends.append(copy)
        return copy

    def drain():
        for copy in sends:
            copy.wait_send()
        sends.clear()

    c0 = c * HALF
    col_a = pl.multiple_of(c0, 128)
    col_b = pl.multiple_of(c0 + GA, 128)
    col_q0 = pl.multiple_of(c0 + GA + GB, 128)
    col_q = pl.multiple_of(c0 + GA + GB + x * GQ, 128)

    w_load = pltpu.make_async_copy(w_ref, W, local_sem.at[0])
    w_load.start()
    own_ab = pltpu.make_async_copy(
        hid_ref.at[:, pl.ds(col_a, GA + GB)], H.at[y, z, :, pl.ds(col_a, GA + GB)], local_sem.at[1]
    )
    own_ab.start()
    own_q = pltpu.make_async_copy(
        hid_ref.at[:, pl.ds(col_q, GQ)], H.at[y, z, :, pl.ds(col_q, GQ)], local_sem.at[2]
    )
    own_q.start()

    barrier = pltpu.get_barrier_semaphore()
    peers = [dict(dc=1)]
    peers += [dict(dx=i, dy=j) for i in range(NX) for j in range(NY) if i or j]
    peers += [dict(dz=k) for k in range(1, NZ)]
    for p in peers:
        pl.semaphore_signal(barrier, inc=1, device_id=dev(**p), device_id_type=MESH)
    pl.semaphore_wait(barrier, len(peers))
    own_ab.wait()
    own_q.wait()

    def blk_a(zz):
        return H.at[:, zz, :, pl.ds(col_a, GA)]

    def blk_b(yy, zz):
        return H.at[yy, zz, :, pl.ds(col_b, GB)]

    def blk_q(zz):
        return H.at[:, zz, :, pl.ds(col_q, GQ)]

    own_a = H.at[y, z, :, pl.ds(col_a, GA)]
    own_qb = H.at[y, z, :, pl.ds(col_q, GQ)]
    first_a = [remote(own_a, own_a, dy=j) for j in (1, 2, 3)]
    first_q = [remote(own_qb, own_qb, dy=j) for j in (1, 2, 3)]

    def both_ways(ref):
        return (remote(ref, ref, dz=1), remote(ref, ref, dz=-1))

    def fan_y(zz):
        return [remote(blk_b(y, zz), blk_b(y, zz), dy=j) for j in (1, 2, 3)]

    def fan_x(zz):
        return [remote(blk_q(zz), blk_q(zz), dx=j) for j in (1, 2, 3)]

    def hand_over(ref):
        return remote(ref, ref, dc=1)

    handed = []
    waiting = []

    def hand_waiting():
        for zz, from_y, from_x in waiting:
            for copy in from_y:
                copy.wait_recv()
            handed.append(hand_over(H.at[:, zz, :, pl.ds(col_b, GB)]))
            for copy in from_x:
                copy.wait_recv()
            handed.append(hand_over(H.at[:, zz, :, pl.ds(col_q0, NX * GQ)]))
        waiting.clear()

    ring_b = both_ways(blk_b(y, z))
    fy = fan_y(z)
    for copy in first_a:
        copy.wait_recv()
    ring_a = both_ways(blk_a(z))
    for copy in first_q:
        copy.wait_recv()
    ring_q = both_ways(blk_q(z))
    fx = fan_x(z)
    handed.append(hand_over(blk_a(z)))
    waiting.append((z, fy, fx))

    def halves(yy, zz, col, n, k):
        cut = n // 256 * 128
        lo = col if k == 0 else pl.multiple_of(col + cut, 128)
        return H.at[yy, zz, :, pl.ds(lo, cut if k == 0 else n - cut)]

    for s in (1, 2, 3):
        now = []
        nb, na, nq = [], [], []
        for k, sign in ((0, 1), (1, -1)):
            zz = wrap(z - sign * s, NZ)
            ring_b[k].wait_recv()
            ref = blk_b(y, zz) if s < 3 else halves(y, zz, col_b, GB, k)
            nb.append(remote(ref, ref, dz=sign))
            fy = fan_y(zz)
            ring_q[k].wait_recv()
            ref = blk_q(zz) if s < 3 else halves(slice(None), zz, col_q, GQ, k)
            nq.append(remote(ref, ref, dz=sign))
            fx = fan_x(zz)
            ring_a[k].wait_recv()
            ref = blk_a(zz) if s < 3 else halves(slice(None), zz, col_a, GA, k)
            na.append(remote(ref, ref, dz=sign))
            handed.append(hand_over(blk_a(zz)))
            now.append((zz, fy, fx))
        hand_waiting()
        waiting.extend(now)
        ring_b, ring_a, ring_q = nb, na, nq

    zz = wrap(z + 4, NZ)
    ring_b[0].wait_recv()
    ring_b[1].wait_recv()
    fy = fan_y(zz)
    ring_q[0].wait_recv()
    ring_q[1].wait_recv()
    fx = fan_x(zz)
    ring_a[0].wait_recv()
    ring_a[1].wait_recv()
    handed.append(hand_over(blk_a(zz)))
    hand_waiting()
    waiting.append((zz, fy, fx))
    hand_waiting()
    for copy in handed:
        copy.wait_recv()
    drain()

    all_copy = pltpu.make_async_copy(H, all_ref, local_sem.at[1])
    all_copy.start()
    w_load.wait()

    KC = 1024
    acc = jnp.zeros((ROWS, VSH), F32)
    for k in range(D // KC):
        h = H[:, :, :, k * KC:(k + 1) * KC].reshape(ROWS, KC)
        acc = acc + jnp.dot(h, W[k * KC:(k + 1) * KC, :], preferred_element_type=F32)
    lt = acc.T
    logits_t[...] = lt

    def lanes(ref4):
        return jnp.concatenate([ref4[i:i + 1, :] for i in range(4)], axis=1)

    targets = lanes(tgt_ref[...])
    first_col = (ctx * 8 + tp) * VSH
    cols = first_col + lax.broadcasted_iota(jnp.int32, (VSH, ROWS), 0)
    matches = cols == targets
    peak = jnp.max(lt, axis=0, keepdims=True)
    local_lse = peak + jnp.log(jnp.sum(jnp.exp(lt - peak), axis=0, keepdims=True))
    picked = jnp.sum(jnp.where(matches, lt, 0.0), axis=0, keepdims=True)
    for i in range(4):
        st_own[0, i:i + 1, :] = local_lse[:, i * 128:(i + 1) * 128]
        st_own[0, 4 + i:5 + i, :] = picked[:, i * 128:(i + 1) * 128]

    def merge(mine, others):
        every = [mine] + others
        top = functools.reduce(jnp.maximum, every)
        total = functools.reduce(jnp.add, [jnp.exp(e - top) for e in every])
        summed = functools.reduce(jnp.add, every)
        row = lax.broadcasted_iota(jnp.int32, (8, 128), 0)
        return jnp.where(row < 4, top + jnp.log(total), summed)

    copy = remote(st_own.at[0], st_core, dc=1)
    copy.wait_recv()
    st = merge(st_own[0], [st_core[...]])
    st_own[1] = st
    group = [(i, j) for i in range(NX) for j in range(NY) if i or j]
    copies = [remote(st_own.at[1], st_xy.at[n], dx=i, dy=j) for n, (i, j) in enumerate(group)]
    for copy in copies:
        copy.wait_recv()
    st = merge(st, [st_xy[n] for n in range(15)])
    st_own[2] = st
    copies = [remote(st_own.at[2], st_z.at[k - 1], dz=k) for k in range(1, NZ)]
    for copy in copies:
        copy.wait_recv()
    st = merge(st, [st_z[n] for n in range(7)])
    lse4 = st[0:4, :]
    logp4 = st[4:8, :] - lse4
    seq4 = seq_ref[...]

    def total_of(v):
        return jnp.sum(jnp.sum(v, axis=1, keepdims=True), axis=0, keepdims=True)

    seq0 = total_of(jnp.where(seq4 == 0, logp4, 0.0))
    seq1 = total_of(jnp.where(seq4 == 1, logp4, 0.0))
    margin = DPO_BETA * ((seq0 - ref_ref[0]) - (seq1 - ref_ref[1]))
    neg = jnp.broadcast_to(-margin, (8, 128))
    loss_ref[...] = jnp.maximum(neg, 0.0) + jnp.log1p(jnp.exp(-jnp.abs(neg)))
    pull = (LOSS_SCALE * DPO_BETA) / (1.0 + jnp.exp(margin))
    coef4 = jnp.where(seq4 == 0, -pull, jnp.where(seq4 == 1, pull, 0.0))
    lse = lanes(lse4)
    coef = lanes(coef4)
    lt = logits_t[...]
    g_t = coef * (matches.astype(F32) - jnp.exp(lt - lse))
    g = g_t.T.astype(BF16)
    G[...] = g
    grad_copy = pltpu.make_async_copy(G, grad_ref, local_sem.at[2])
    grad_copy.start()

    def partial_of(xx, cc, off, n):
        start = pl.multiple_of((xx * 2 + cc) * 1024 + off, 128)
        return lax.dot_general(
            G[...], W[pl.ds(start, n), :], (((1,), (1,)), ((), ())), preferred_element_type=F32
        ).reshape(NY, NZ, 16, n)

    part_x = (psx, plx, sx, 0, SX)
    part_y = (psy, ply, sy, SX, SY)
    part_z = (psz, plz, sz, SX + SY, SZ)
    order = [(part_x, 2)] + [(part_z, j) for j in range(4)] + [(part_y, j) for j in range(4)]
    order += [(part_x, 1), (part_x, 3), (part_x, 0)]
    swaps = []
    for (ps, plnd, _, off, n), j in order:
        xx = wrap(x + j, NX)
        ps[xx] = partial_of(xx, 1 - c, off, n).astype(BF16)
        swaps.append(remote(ps.at[xx], plnd.at[xx], dc=1))

    def own_chunk(i):
        (_, plnd, s, off, n), j = order[i]
        xx = wrap(x + j, NX)
        mine = partial_of(xx, c, off, n)
        swaps[i].wait_recv()
        s[xx] = (mine + plnd[xx].astype(F32)).astype(BF16)

    def send_x(j):
        return remote(sx.at[wrap(x + j, NX)], lx1.at[j - 1], dx=j)

    def add(ref, idx, *others):
        total = ref[idx].astype(F32)
        for o in others:
            total = total + o.astype(F32)
        return total.astype(BF16)

    own_chunk(0)
    cx = {2: send_x(2)}
    for i in range(1, 5):
        own_chunk(i)
    zh = SZ // 2
    zr = remote(sz.at[:, :, wrap(z + 4, NZ), :, 0:zh], lz1h.at[0], dz=1)
    zl = remote(sz.at[:, :, wrap(z + 4, NZ), :, zh:SZ], lz1h.at[1], dz=-1)
    for i in range(5, 9):
        own_chunk(i)
    cy = [remote(sy.at[:, wrap(y + j, NY)], ly1.at[j - 1], dy=j) for j in (1, 2, 3)]

    def z_step(k, zr, zl):
        right, left = wrap(z + k, NZ), wrap(z - k, NZ)
        zr.wait_recv()
        zl.wait_recv()
        if k == 3:
            r_in, l_in = lz1h[0], lz1h[1]
            sz[:, :, right, :, 0:zh] = (sz[:, :, right, :, 0:zh].astype(F32) + r_in.astype(F32)).astype(BF16)
            sz[:, :, left, :, zh:SZ] = (sz[:, :, left, :, zh:SZ].astype(F32) + l_in.astype(F32)).astype(BF16)
        else:
            n = 2 - k
            sz[:, :, right] = (sz[:, :, right].astype(F32) + lz1[n, 0].astype(F32)).astype(BF16)
            sz[:, :, left] = (sz[:, :, left].astype(F32) + lz1[n, 1].astype(F32)).astype(BF16)
        n = 3 - k
        return (
            remote(sz.at[:, :, right], lz1.at[n, 0], dz=1),
            remote(sz.at[:, :, left], lz1.at[n, 1], dz=-1),
        )

    zr, zl = z_step(3, zr, zl)
    own_chunk(9)
    cx[1] = send_x(1)
    own_chunk(10)
    cx[3] = send_x(3)
    own_chunk(11)
    zr, zl = z_step(2, zr, zl)
    zr, zl = z_step(1, zr, zl)

    for j in (1, 2, 3):
        cx[j].wait_recv()
    for yy in range(NY):
        sx[x, yy] = add(sx, (x, yy), lx1[0, yy], lx1[1, yy], lx1[2, yy])
    cx = [remote(sx.at[x, wrap(y + j, NY)], lx2.at[j - 1], dy=j) for j in (1, 2, 3)]
    for copy in cy:
        copy.wait_recv()
    for xx in range(NX):
        sy[xx, y] = add(sy, (xx, y), ly1[0, xx], ly1[1, xx], ly1[2, xx])
    cy = [remote(sy.at[wrap(x + j, NX), y], ly2.at[j - 1], dx=j) for j in (1, 2, 3)]
    zr.wait_recv()
    zl.wait_recv()
    for xx in range(NX):
        sz[xx, :, z] = (
            sz[xx, :, z].astype(F32) + lz1[2, 0, xx].astype(F32) + lz1[2, 1, xx].astype(F32)
        ).astype(BF16)
    cz = [remote(sz.at[wrap(x + j, NX), :, z], lz2.at[j - 1], dx=j) for j in (1, 2, 3)]

    for copy in cx:
        copy.wait_recv()
    rx2[...] = add(sx, (x, y), lx2[0], lx2[1], lx2[2])
    cx = [remote(rx2.at[wrap(z + k, NZ)], lx3.at[k - 1], dz=k) for k in range(1, NZ)]
    for copy in cy:
        copy.wait_recv()
    ry2[...] = add(sy, (x, y), ly2[0], ly2[1], ly2[2])
    cy = [remote(ry2.at[wrap(z + k, NZ)], ly3.at[k - 1], dz=k) for k in range(1, NZ)]
    for copy in cz:
        copy.wait_recv()
    sz[x, :, z] = (
        sz[x, :, z].astype(F32) + lz2[0].astype(F32) + lz2[1].astype(F32) + lz2[2].astype(F32)
    ).astype(BF16)
    cz = [remote(sz.at[x, wrap(y + j, NY), z], lz3.at[j - 1], dy=j) for j in (1, 2, 3)]

    for copy in cx:
        copy.wait_recv()
    total = rx2[z].astype(F32)
    for k in range(7):
        total = total + lx3[k].astype(F32)
    dh_ref[:, 0:SX] = total.astype(BF16)
    for copy in cy:
        copy.wait_recv()
    total = ry2[z].astype(F32)
    for k in range(7):
        total = total + ly3[k].astype(F32)
    dh_ref[:, SX:SX + SY] = total.astype(BF16)
    for copy in cz:
        copy.wait_recv()
    total = sz[x, y, z].astype(F32)
    for k in range(3):
        total = total + lz3[k].astype(F32)
    dh_ref[:, SX + SY:] = total.astype(BF16)

    drain()
    all_copy.wait()
    grad_copy.wait()


def on_device(hidden, weight, targets, row_seq, ref_logp):
    vmem = pl.BlockSpec(memory_space=pltpu.VMEM)
    hbm = pl.BlockSpec(memory_space=pl.ANY)
    smem = pl.BlockSpec(memory_space=pltpu.SMEM)

    def v16(*shape):
        return pltpu.VMEM(shape, BF16)

    chunks = [v16(NX, NY, NZ, 16, n) for n in (SX, SY, SZ)]
    all_rows, grad, loss, d_hidden = pl.pallas_call(
        fused_kernel,
        out_shape=(
            jax.ShapeDtypeStruct((NY, NZ, 16, D), BF16),
            jax.ShapeDtypeStruct((ROWS, VSH), BF16),
            jax.ShapeDtypeStruct((8, 128), F32),
            jax.ShapeDtypeStruct((16, 1024), BF16),
        ),
        in_specs=[hbm, hbm, vmem, vmem, smem],
        out_specs=(hbm, hbm, vmem, vmem),
        scratch_shapes=[
            v16(NY, NZ, 16, D),
            v16(D, VSH),
            pltpu.VMEM((VSH, ROWS), F32),
            v16(ROWS, VSH),
            pltpu.VMEM((3, 8, 128), F32),
            pltpu.VMEM((8, 128), F32),
            pltpu.VMEM((15, 8, 128), F32),
            pltpu.VMEM((7, 8, 128), F32),
            *chunks, *chunks, *chunks,
            v16(3, NY, NZ, 16, SX), v16(3, NZ, 16, SX), v16(7, 16, SX),
            v16(3, NX, NZ, 16, SY), v16(3, NZ, 16, SY), v16(7, 16, SY),
            v16(2, NX, NY, 16, SZ // 2), v16(3, 2, NX, NY, 16, SZ), v16(3, NY, 16, SZ), v16(3, 16, SZ),
            v16(NZ, 16, SX), v16(NZ, 16, SY),
            pltpu.SemaphoreType.DMA((3,)),
            pltpu.SemaphoreType.DMA((N_SEM,)),
            pltpu.SemaphoreType.DMA((N_SEM,)),
        ],
        compiler_params=pltpu.CompilerParams(
            collective_id=0, has_side_effects=True, vmem_limit_bytes=56 * 2**20
        ),
        cost_estimate=pl.CostEstimate(flops=2 * 2 * ROWS * D * VSH, bytes_accessed=2 * D * VSH, transcendentals=0),
    )(hidden, weight, targets.reshape(4, 128), row_seq.reshape(4, 128), ref_logp)
    d_weight = lax.dot_general(
        all_rows.reshape(ROWS, D), grad, (((0,), (0,)), ((), ())), preferred_element_type=F32
    ).astype(BF16)
    return (loss[0, 0], d_hidden, d_weight)


def solution(mesh):
    placed = (P("ctx", None), P(None, ("ctx", "tp")), P(), P(), P())
    return jax.shard_map(
        on_device,
        mesh=mesh,
        in_specs=placed,
        out_specs=(P(), P("ctx", "tp"), P(None, ("ctx", "tp"))),
        check_vma=False,
    )
```

time: 561 us -> 115 us (0.20)
  waiting for transfers between devices: 358 us -> 0 us
  blocking collectives: 147 us -> 0 us
  Pallas kernels: 0 us -> 99.8 us
  between operations: 17.6 us -> 0.64 us
  matrix products: 27.6 us -> 10.7 us
  local copies, waits for them, and re-layouts: 9.22 us -> 1.81 us
    reduce_scatter x2 -> x0, waiting for transfers between devices: 253 us -> none  [the longest x1 203 us: on_device(): d_hidden = lax.psum_scatter(narrow, 'ctx', scatter_dimension=0, tiled=True)]
    all_gather x1 -> x0, waiting for transfers between devices: 104 us -> none  [on_device(): all_rows = lax.all_gather(hidden, 'ctx', axis=0, tiled=True)]
    pallas_call x0 -> x1, Pallas kernels: none -> 99.8 us  [on_device(): pl.pallas_call(fused_kernel, out_shape=(jax.ShapeDtypeStruct((NY, NZ, 16,...]
    pmax x1 -> x0, blocking collectives: 73.9 us -> none  [on_device(): row_peak = lax.pmax(local_peak, ('ctx', 'tp'))]
    psum x1 -> x0, blocking collectives: 73.3 us -> none  [on_device(): row_total, target_logit = lax.psum((local_total, picked), ('ctx', 'tp'))]
    dot_general x3 -> x1, matrix products: 27.6 us -> 10.7 us  [on_device(): lax.dot_general(all_rows.reshape(ROWS, D), grad, (((0,), (0,)), ((), ()))...]
    unnamed x7 -> x3, local copies, waits for them, and re-layouts: 8.63 us -> 0.62 us
  transfers between devices with their start and end apart: 3 -> 0, of which waited for: 3 -> 0; matrix products, arithmetic and copies ran while one was open for 3% -> 0% of each run, Pallas kernels for 0% -> 0%
where the time goes in v1:
time: 115 us; the launch traced here: 113 us
  Pallas kernels  99.8 us (87%)
  matrix products  10.7 us (9%)
  local copies, waits for them, and re-layouts  1.81 us (2%)
    pallas_call x1, Pallas kernels, on_device(): pl.pallas_call(fused_kernel, out_shape=(jax.ShapeDtypeStruct((NY, NZ, 16,...  99.8 us
    dot_general x1, matrix products, on_device(): lax.dot_general(all_rows.reshape(ROWS, D), grad, (((0,), (0,)), ((), ()))...  10.7 us

profile of v1, /device:TPU:6, one launch (start us, length us, event | category | flops | bytes accessed | tf_op | source)
XLA Modules:
  0.0 113.0 jit_solution(4792228126757088959)
XLA Ops:
  0.6 99.8 %shard_map.76 = (bf16[4,8,16,8192]{3,2,1,0:T(8,128)(2,1)}, bf16[512,384]{1,0:T(8,128)(2,1)}, f32[8,128]{1,0:T(8,128)}, bf16[16,1024]{1,0:T(8,128)(2,1)}) custom-call(bf16[16,8192]{1,0:T(8,128)(2,1)} %hid_ref.1, bf16[8192,384]{1,0:T(8,128)(2,1)} %w_ref.1, s32[4,128]{1,0:T(4,128)} %bitcast.6, s32[4,128]{1,0:T(4,128)} %bitcast.7, f32[2]{0:T(128)} %ref_ref.1), custom_call_target="tpu_custom_call" | custom-call | flops 6442450944 | bytes 6291456 | tf_op jit(solution)/shard_map/pallas_call | solution.py:405
  100.5 1.2 %slice.3 = f32[1,1]{1,0:T(1,128)} slice(f32[8,128]{1,0:T(8,128)} %get-tuple-element.7), slice={[0:1], [0:1]} | slice | bytes 8 | tf_op jit(solution)/shard_map/slice | solution.py:441
  101.7 0.0 copy-start
  101.7 10.7 %convolution_convert_fusion = bf16[8192,384]{1,0:T(8,128)(2,1)} fusion(bf16[512,8192]{1,0:T(8,128)(2,1)} %bitcast.8, bf16[512,384]{1,0:T(8,128)(2,1)} %get-tuple-element.10), kind=kOutput, calls=%fused_computation | convolution fusion | flops 3224371200 | bytes 15073280 | tf_op jit(solution)/shard_map/dot_general | solution.py:438
  112.3 0.0 copy-done
  112.3 0.6 copy.9
Async XLA Ops:
  101.7 10.7 %copy-start = (bf16[16,1024]{1,0:T(8,128)(2,1)S(1)}, bf16[16,1024]{1,0:T(8,128)(2,1)}, u32[]{:S(2)}) copy-start(bf16[16,1024]{1,0:T(8,128)(2,1)} %get-tuple-element.15) | copy-start | bytes 98308

commit v2 on v1

v2 whole, which is shorter than its diff:
```python
import functools

import jax
import jax.numpy as jnp
from jax import lax
from jax.experimental import pallas as pl
from jax.experimental.pallas import tpu as pltpu
from jax.sharding import PartitionSpec as P

MESH = pl.DeviceIdType.MESH
F32 = jnp.float32
BF16 = jnp.bfloat16

DPO_BETA = 0.01
LOSS_SCALE = 1024.0

NX, NY, NZ = 4, 4, 8
ROWS = 512
D = 8192
VSH = 384
HALF = 4096

GA, GB, GQ = 1024, 1536, 384
SX, SY, SZ = 384, 384, 256

N_SEM = 200

KC = 1024


def fused_kernel(
    hid_ref, w_ref, tgt_ref, seq_ref, ref_ref,
    dw_ref, loss_ref, dh_ref,
    H, W, L, logits_t, G,
    st_own, st_core, st_xy, st_z,
    psx, psy, psz, plx, ply, plz, sx, sy, sz,
    hx, lx1, lx2, lx3, hy, ly1, ly2, ly3, lz3s, lz4s, lz1, lz2, lz5, lz3,
    local_sem, ssem, rsem,
):
    ctx = lax.axis_index("ctx")
    tp = lax.axis_index("tp")
    y = ctx // NZ
    z = lax.rem(ctx, NZ)
    x = tp // 2
    c = lax.rem(tp, 2)

    def wrap(v, n):
        return lax.rem(v + n, n)

    def dev(dy=0, dz=0, dx=0, dc=0):
        yy = wrap(y + dy, NY) if dy else y
        zz = wrap(z + dz, NZ) if dz else z
        xx = wrap(x + dx, NX) if dx else x
        cc = 1 - c if dc else c
        return (yy * NZ + zz, xx * 2 + cc)

    counter = [0]
    sends = []

    def remote(src, dst, **d):
        i = counter[0]
        counter[0] += 1
        copy = pltpu.make_async_remote_copy(
            src_ref=src, dst_ref=dst, send_sem=ssem.at[i], recv_sem=rsem.at[i],
            device_id=dev(**d), device_id_type=MESH,
        )
        copy.start()
        sends.append(copy)
        return copy

    def rx(copy):
        copy.wait_recv()

    def drain():
        for copy in sends:
            copy.wait_send()
        sends.clear()

    c0 = c * HALF
    col_a = pl.multiple_of(c0, 128)
    col_b = pl.multiple_of(c0 + GA, 128)
    col_q0 = pl.multiple_of(c0 + GA + GB, 128)
    col_q = pl.multiple_of(c0 + GA + GB + x * GQ, 128)

    w_load = pltpu.make_async_copy(w_ref, W, local_sem.at[0])
    w_load.start()
    own_ab = pltpu.make_async_copy(
        hid_ref.at[:, pl.ds(col_a, GA + GB)], H.at[y, z, :, pl.ds(col_a, GA + GB)], local_sem.at[1]
    )
    own_ab.start()
    own_q = pltpu.make_async_copy(
        hid_ref.at[:, pl.ds(col_q, GQ)], H.at[y, z, :, pl.ds(col_q, GQ)], local_sem.at[2]
    )
    own_q.start()

    barrier = pltpu.get_barrier_semaphore()
    peers = [dict(dc=1)]
    peers += [dict(dx=i, dy=j) for i in range(NX) for j in range(NY) if i or j]
    peers += [dict(dz=k) for k in range(1, NZ)]
    for p in peers:
        pl.semaphore_signal(barrier, inc=1, device_id=dev(**p), device_id_type=MESH)
    pl.semaphore_wait(barrier, len(peers))
    own_ab.wait()
    own_q.wait()

    def blk_a(zz):
        return H.at[:, zz, :, pl.ds(col_a, GA)]

    def blk_b(yy, zz):
        return H.at[yy, zz, :, pl.ds(col_b, GB)]

    def blk_q(zz):
        return H.at[:, zz, :, pl.ds(col_q, GQ)]

    own_a = H.at[y, z, :, pl.ds(col_a, GA)]
    own_qb = H.at[y, z, :, pl.ds(col_q, GQ)]
    first_a = [remote(own_a, own_a, dy=j) for j in (1, 2, 3)]
    first_q = [remote(own_qb, own_qb, dy=j) for j in (1, 2, 3)]

    def both_ways(ref):
        return (remote(ref, ref, dz=1), remote(ref, ref, dz=-1))

    def fan_y(zz):
        return [remote(blk_b(y, zz), blk_b(y, zz), dy=j) for j in (1, 2, 3)]

    def fan_x(zz):
        return [remote(blk_q(zz), blk_q(zz), dx=j) for j in (1, 2, 3)]

    def hand_over(ref):
        return remote(ref, ref, dc=1)

    handed = {}
    arrivals = {}

    def hand_on(key, zz):
        from_y, from_x = arrivals.pop(key)
        for copy in from_y:
            rx(copy)
        handed[key].append(hand_over(H.at[:, zz, :, pl.ds(col_b, GB)]))
        for copy in from_x:
            rx(copy)
        handed[key].append(hand_over(H.at[:, zz, :, pl.ds(col_q0, NX * GQ)]))

    def logits_of(keys):
        zs = [wrap(z - sign * st, NZ) for st, sign in keys]
        for key in keys:
            for copy in handed[key]:
                rx(copy)
        def step(k, acc):
            at = pl.ds(pl.multiple_of(k * KC, KC), KC)
            h = jnp.concatenate([H[yy, zz, :, at] for zz in zs for yy in range(NY)], axis=0)
            return acc + jnp.dot(h, W[at, :], preferred_element_type=F32)

        acc = lax.fori_loop(0, D // KC, step, jnp.zeros((64 * len(zs), VSH), F32))
        acc = acc.reshape(len(zs), NY, 16, VSH)
        for n, zz in enumerate(zs):
            L[:, zz] = acc[n]

    ring_b = both_ways(blk_b(y, z))
    fy = fan_y(z)
    for copy in first_a:
        rx(copy)
    ring_a = both_ways(blk_a(z))
    for copy in first_q:
        rx(copy)
    ring_q = both_ways(blk_q(z))
    fx = fan_x(z)
    handed[0, 1] = [hand_over(blk_a(z))]
    arrivals[0, 1] = (fy, fx)

    def halves(yy, zz, col, n, k):
        cut = n // 256 * 128
        lo = col if k == 0 else pl.multiple_of(col + cut, 128)
        return H.at[yy, zz, :, pl.ds(lo, cut if k == 0 else n - cut)]

    for s in (1, 2, 3):
        nb, na, nq = [], [], []
        for k, sign in ((0, 1), (1, -1)):
            zz = wrap(z - sign * s, NZ)
            rx(ring_b[k])
            ref = blk_b(y, zz) if s < 3 else halves(y, zz, col_b, GB, k)
            nb.append(remote(ref, ref, dz=sign))
            fy = fan_y(zz)
            rx(ring_q[k])
            ref = blk_q(zz) if s < 3 else halves(slice(None), zz, col_q, GQ, k)
            nq.append(remote(ref, ref, dz=sign))
            fx = fan_x(zz)
            rx(ring_a[k])
            ref = blk_a(zz) if s < 3 else halves(slice(None), zz, col_a, GA, k)
            na.append(remote(ref, ref, dz=sign))
            handed[s, sign] = [hand_over(blk_a(zz))]
            arrivals[s, sign] = (fy, fx)
        for key in list(arrivals):
            if key[0] < s:
                hand_on(key, wrap(z - key[1] * key[0], NZ))
        if s == 2:
            w_load.wait()
        if s == 3:
            logits_of([(1, 1), (1, -1)])
        ring_b, ring_a, ring_q = nb, na, nq

    zz = wrap(z + 4, NZ)
    rx(ring_b[0])
    rx(ring_b[1])
    fy = fan_y(zz)
    rx(ring_q[0])
    rx(ring_q[1])
    fx = fan_x(zz)
    rx(ring_a[0])
    rx(ring_a[1])
    handed[4, -1] = [hand_over(blk_a(zz))]
    arrivals[4, -1] = (fy, fx)
    hand_on((3, 1), wrap(z - 3, NZ))
    hand_on((3, -1), wrap(z + 3, NZ))
    logits_of([(2, 1), (2, -1)])
    hand_on((4, -1), zz)
    logits_of([(3, 1), (3, -1)])
    logits_of([(0, 1), (4, -1)])
    drain()

    lt = L[...].reshape(ROWS, VSH).T
    logits_t[...] = lt

    def lanes(ref4):
        return jnp.concatenate([ref4[i:i + 1, :] for i in range(4)], axis=1)

    targets = lanes(tgt_ref[...])
    first_col = (ctx * 8 + tp) * VSH
    cols = first_col + lax.broadcasted_iota(jnp.int32, (VSH, ROWS), 0)
    matches = cols == targets
    peak = jnp.max(lt, axis=0, keepdims=True)
    local_lse = peak + jnp.log(jnp.sum(jnp.exp(lt - peak), axis=0, keepdims=True))
    picked = jnp.sum(jnp.where(matches, lt, 0.0), axis=0, keepdims=True)
    for i in range(4):
        st_own[0, i:i + 1, :] = local_lse[:, i * 128:(i + 1) * 128]
        st_own[0, 4 + i:5 + i, :] = picked[:, i * 128:(i + 1) * 128]

    def merge(mine, others):
        every = [mine] + others
        top = functools.reduce(jnp.maximum, every)
        total = functools.reduce(jnp.add, [jnp.exp(e - top) for e in every])
        summed = functools.reduce(jnp.add, every)
        row = lax.broadcasted_iota(jnp.int32, (8, 128), 0)
        return jnp.where(row < 4, top + jnp.log(total), summed)

    copy = remote(st_own.at[0], st_core, dc=1)
    rx(copy)
    st = merge(st_own[0], [st_core[...]])
    st_own[1] = st
    group = [(i, j) for i in range(NX) for j in range(NY) if i or j]
    copies = [remote(st_own.at[1], st_xy.at[n], dx=i, dy=j) for n, (i, j) in enumerate(group)]
    for copy in copies:
        rx(copy)
    st = merge(st, [st_xy[n] for n in range(15)])
    st_own[2] = st
    copies = [remote(st_own.at[2], st_z.at[k - 1], dz=k) for k in range(1, NZ)]
    for copy in copies:
        rx(copy)
    st = merge(st, [st_z[n] for n in range(7)])
    lse4 = st[0:4, :]
    logp4 = st[4:8, :] - lse4
    seq4 = seq_ref[...]

    def total_of(v):
        return jnp.sum(jnp.sum(v, axis=1, keepdims=True), axis=0, keepdims=True)

    seq0 = total_of(jnp.where(seq4 == 0, logp4, 0.0))
    seq1 = total_of(jnp.where(seq4 == 1, logp4, 0.0))
    margin = DPO_BETA * ((seq0 - ref_ref[0]) - (seq1 - ref_ref[1]))
    neg = jnp.broadcast_to(-margin, (8, 128))
    loss_ref[...] = jnp.maximum(neg, 0.0) + jnp.log1p(jnp.exp(-jnp.abs(neg)))
    pull = (LOSS_SCALE * DPO_BETA) / (1.0 + jnp.exp(margin))
    coef4 = jnp.where(seq4 == 0, -pull, jnp.where(seq4 == 1, pull, 0.0))
    lse = lanes(lse4)
    coef = lanes(coef4)
    lt = logits_t[...]
    g_t = coef * (matches.astype(F32) - jnp.exp(lt - lse))
    g = g_t.T.astype(BF16)
    G[...] = g

    def weight_grad(first, last):
        n = 512

        def step(i, carry):
            at = pl.ds(pl.multiple_of(i * n, n), n)
            h = H[:, :, :, at].reshape(ROWS, n)
            dw_ref[at, :] = lax.dot_general(
                h, G[...], (((0,), (0,)), ((), ())), preferred_element_type=F32
            ).astype(BF16)
            return carry

        lax.fori_loop(first, last, step, 0)

    def product(rows, xx, cc, off, n):
        start = pl.multiple_of((xx * 2 + cc) * 1024 + off, 128)
        return lax.dot_general(
            rows, W[pl.ds(start, n), :], (((1,), (1,)), ((), ())), preferred_element_type=F32
        )

    def x_dot(j, cc):
        return [product(G[...], wrap(x + j, NX), cc, 0, SX).reshape(NY, NZ, 16, SX)]

    def y_dot(j, cc):
        rows = G[pl.ds(pl.multiple_of(wrap(y + j, NY) * 128, 128), 128), :]
        return [product(rows, xx, cc, SX, SY).reshape(NZ, 16, SY) for xx in range(NX)]

    def z_dot(j, cc):
        p = product(G[...], j, cc, SX + SY, SZ).reshape(NY, NZ, 16, SZ)
        return [p[:, zz] for zz in range(NZ)]

    def places(part, j):
        if part == "x":
            return [(wrap(x + j, NX),)], (wrap(x + j, NX),)
        if part == "y":
            return [(wrap(y + j, NY), xx) for xx in range(NX)], (wrap(y + j, NY),)
        return [(zz, j) for zz in range(NZ)], (slice(None), j)

    parts = {"x": (x_dot, psx, plx, sx), "y": (y_dot, psy, ply, sy), "z": (z_dot, psz, plz, sz)}
    swaps = {}

    def give(part, j):
        dot, ps, land, _ = parts[part]
        idx, whole = places(part, j)
        for at, p in zip(idx, dot(j, 1 - c)):
            ps[at] = p.astype(BF16)
        swaps[part, j] = remote(ps.at[whole], land.at[whole], dc=1)

    def keep(part, j, extra=None):
        dot, _, land, s = parts[part]
        idx, _ = places(part, j)
        mine = dot(j, c)
        rx(swaps[part, j])
        for at, p in zip(idx, mine):
            s[at] = (p + land[at].astype(F32)).astype(BF16)

    def bump(ref, at, *others):
        total = ref[at].astype(F32)
        for o in others:
            total = total + o.astype(F32)
        ref[at] = total.astype(BF16)

    lo, hi = slice(0, 2), slice(2, 4)

    def send_halves(s, h, me, n, **d):
        (axis,) = d
        far = wrap(me + 2, n)
        return (
            remote(s.at[far, lo], h.at[0], **{axis: 1}),
            remote(s.at[far, hi], h.at[1], **{axis: -1}),
        )

    def send_near(s, h, land, me, n, halves_in, side, axis):
        at = wrap(me + side, n)
        k = 0 if side == 1 else 1
        rx(halves_in[k])
        for i in (0, 1):
            bump(s, (at, 2 * k + i), h[k, i])
        return remote(s.at[at], land.at[k], **{axis: side})

    give("x", 2)
    give("y", 2)
    for j in range(4):
        give("z", j)
    keep("x", 2)
    xh = send_halves(sx, hx, x, NX, dx=0)
    keep("y", 2)
    yh = send_halves(sy, hy, y, NY, dy=0)
    give("x", 1)
    give("x", 3)
    for j in range(4):
        keep("z", j)

    def zat(k):
        return wrap(z + k, NZ)

    z3r = remote(sz.at[zat(3)], lz3s.at[0], dz=1)
    z3l = remote(sz.at[zat(-3)], lz3s.at[1], dz=-1)
    z4l = remote(sz.at[zat(4), lo], lz4s.at[0], dz=-2)
    z4r = remote(sz.at[zat(4), hi], lz4s.at[1], dz=2)
    z1r = remote(sz.at[zat(1)], lz1.at[0], dz=1)
    z1l = remote(sz.at[zat(-1)], lz1.at[1], dz=-1)
    give("y", 1)
    give("y", 3)
    give("x", 0)
    give("y", 0)
    weight_grad(0, 2)
    keep("x", 1)
    xr = send_near(sx, hx, lx1, x, NX, xh, 1, "dx")
    keep("x", 3)
    xl = send_near(sx, hx, lx1, x, NX, xh, -1, "dx")
    keep("y", 1)
    yr = send_near(sy, hy, ly1, y, NY, yh, 1, "dy")
    keep("y", 3)
    yl = send_near(sy, hy, ly1, y, NY, yh, -1, "dy")
    keep("x", 0)
    keep("y", 0)
    rx(z3r)
    rx(z3l)
    rx(z4l)
    rx(z4r)
    for i in range(NX):
        bump(sz, (zat(-2), i), lz3s[1, i], *([lz4s[0, i]] if i < 2 else []))
    z2l = remote(sz.at[zat(-2)], lz2.at[0], dz=-2)
    for i in range(NX):
        bump(sz, (zat(2), i), lz3s[0, i], *([lz4s[1, i - 2]] if i >= 2 else []))
    z2r = remote(sz.at[zat(2)], lz2.at[1], dz=2)
    weight_grad(2, 10)

    rx(xr)
    rx(xl)
    for yy in range(NY):
        bump(sx, (x, yy), lx1[0, yy], lx1[1, yy])
    cx = [remote(sx.at[x, wrap(y + j, NY)], lx2.at[j - 1], dy=j) for j in (1, 2, 3)]
    rx(yr)
    rx(yl)
    for xx in range(NX):
        bump(sy, (y, xx), ly1[0, xx], ly1[1, xx])
    cy = [remote(sy.at[y, wrap(x + j, NX)], ly2.at[j - 1], dx=j) for j in (1, 2, 3)]
    weight_grad(10, 12)
    for copy in (z1r, z1l, z2l, z2r):
        rx(copy)
    for xx in range(NX):
        bump(sz, (z, xx), lz1[0, xx], lz1[1, xx], lz2[0, xx], lz2[1, xx])
    cz = [remote(sz.at[z, wrap(x + j, NX)], lz5.at[j - 1], dx=j) for j in (1, 2, 3)]

    for copy in cx:
        rx(copy)
    bump(sx, (x, y), lx2[0], lx2[1], lx2[2])
    cx = [remote(sx.at[x, y, zat(k)], lx3.at[k - 1], dz=k) for k in range(1, NZ)]
    for copy in cy:
        rx(copy)
    bump(sy, (y, x), ly2[0], ly2[1], ly2[2])
    cy = [remote(sy.at[y, x, zat(k)], ly3.at[k - 1], dz=k) for k in range(1, NZ)]
    for copy in cz:
        rx(copy)
    bump(sz, (z, x), lz5[0], lz5[1], lz5[2])
    cz = [remote(sz.at[z, x, wrap(y + j, NY)], lz3.at[j - 1], dy=j) for j in (1, 2, 3)]
    weight_grad(12, 16)
    for copy in cx:
        rx(copy)
    total = sx[x, y, z].astype(F32)
    for k in range(7):
        total = total + lx3[k].astype(F32)
    dh_ref[:, 0:SX] = total.astype(BF16)
    for copy in cy:
        rx(copy)
    total = sy[y, x, z].astype(F32)
    for k in range(7):
        total = total + ly3[k].astype(F32)
    dh_ref[:, SX:SX + SY] = total.astype(BF16)
    for copy in cz:
        rx(copy)
    total = sz[z, x, y].astype(F32)
    for k in range(3):
        total = total + lz3[k].astype(F32)
    dh_ref[:, SX + SY:] = total.astype(BF16)

    drain()


def run_kernel(hidden, weight, targets, row_seq, ref_logp):
    vmem = pl.BlockSpec(memory_space=pltpu.VMEM)
    hbm = pl.BlockSpec(memory_space=pl.ANY)
    smem = pl.BlockSpec(memory_space=pltpu.SMEM)

    def v16(*shape):
        return pltpu.VMEM(shape, BF16)

    chunks = [v16(NX, NY, NZ, 16, SX), v16(NY, NX, NZ, 16, SY), v16(NZ, NX, NY, 16, SZ)]
    return pl.pallas_call(
        fused_kernel,
        out_shape=(
            pltpu.VMEM((D, VSH), BF16),
            pltpu.VMEM((8, 128), F32),
            pltpu.VMEM((16, 1024), BF16),
        ),
        in_specs=[hbm, hbm, vmem, vmem, smem],
        out_specs=(vmem, vmem, vmem),
        scratch_shapes=[
            v16(NY, NZ, 16, D),
            v16(D, VSH),
            pltpu.VMEM((NY, NZ, 16, VSH), F32),
            pltpu.VMEM((VSH, ROWS), F32),
            v16(ROWS, VSH),
            pltpu.VMEM((3, 8, 128), F32),
            pltpu.VMEM((8, 128), F32),
            pltpu.VMEM((15, 8, 128), F32),
            pltpu.VMEM((7, 8, 128), F32),
            *chunks, *chunks, *chunks,
            v16(2, 2, NZ, 16, SX), v16(2, NY, NZ, 16, SX), v16(3, NZ, 16, SX), v16(7, 16, SX),
            v16(2, 2, NZ, 16, SY), v16(2, NX, NZ, 16, SY), v16(3, NZ, 16, SY), v16(7, 16, SY),
            v16(2, NX, NY, 16, SZ), v16(2, 2, NY, 16, SZ), v16(2, NX, NY, 16, SZ),
            v16(2, NX, NY, 16, SZ), v16(3, NY, 16, SZ), v16(3, 16, SZ),
            pltpu.SemaphoreType.DMA((3,)),
            pltpu.SemaphoreType.DMA((N_SEM,)),
            pltpu.SemaphoreType.DMA((N_SEM,)),
        ],
        compiler_params=pltpu.CompilerParams(
            collective_id=0, has_side_effects=True, vmem_limit_bytes=52 * 2**20
        ),
        cost_estimate=pl.CostEstimate(flops=2 * 2 * ROWS * D * VSH, bytes_accessed=2 * D * VSH, transcendentals=0),
    )(hidden, weight, targets.reshape(4, 128), row_seq.reshape(4, 128), ref_logp)


def on_device(hidden, weight, targets, row_seq, ref_logp):
    dw, loss, dh = run_kernel(hidden, weight, targets, row_seq, ref_logp)

    def leave(dw_ref, loss_ref, dh_ref, dw_out, loss_out, dh_out, sem):
        copy = pltpu.make_async_copy(dw_ref, dw_out, sem.at[0])
        copy.start()
        loss_out[0] = loss_ref[0, 0]
        dh_out[...] = dh_ref[...]
        copy.wait()

    vmem = pl.BlockSpec(memory_space=pltpu.VMEM)
    d_weight, dpo_loss, d_hidden = pl.pallas_call(
        leave,
        out_shape=(
            jax.ShapeDtypeStruct((D, VSH), BF16),
            jax.ShapeDtypeStruct((1,), F32),
            jax.ShapeDtypeStruct((16, 1024), BF16),
        ),
        in_specs=[vmem, vmem, vmem],
        out_specs=(pl.BlockSpec(memory_space=pl.ANY), pl.BlockSpec(memory_space=pltpu.SMEM), vmem),
        scratch_shapes=[pltpu.SemaphoreType.DMA((1,))],
        compiler_params=pltpu.CompilerParams(has_side_effects=True, vmem_limit_bytes=16 * 2**20),
    )(dw, loss, dh)
    return (dpo_loss[0], d_hidden, d_weight)


def solution(mesh):
    placed = (P("ctx", None), P(None, ("ctx", "tp")), P(), P(), P())
    return jax.shard_map(
        on_device,
        mesh=mesh,
        in_specs=placed,
        out_specs=(P(), P("ctx", "tp"), P(None, ("ctx", "tp"))),
        check_vma=False,
    )
```

time: 115 us -> 97.8 us (0.85)
  matrix products: 10.7 us -> 0 us
  Pallas kernels: 99.8 us -> 96 us
  local copies, waits for them, and re-layouts: 1.81 us -> 0 us
    dot_general x1 -> x0, matrix products: 10.7 us -> none  [on_device(): lax.dot_general(all_rows.reshape(ROWS, D), grad, (((0,), (0,)), ((), ()))...]
    pallas_call x1 -> x2, Pallas kernels: 99.8 us -> 96 us  [the longest x1 92.7 us: run_kernel(): pl.pallas_call(fused_kernel, out_shape=(pltpu.VMEM((D, VSH), BF16), pltpu...]
    slice x1 -> x0, local copies, waits for them, and re-layouts: 1.19 us -> none  [on_device(): return (loss[0, 0], d_hidden, d_weight)]
where the time goes in v2:
time: 97.8 us; the launch traced here: 96.6 us
  Pallas kernels  96 us (98%)
    pallas_call x1, Pallas kernels, run_kernel(): pl.pallas_call(fused_kernel, out_shape=(pltpu.VMEM((D, VSH), BF16), pltpu...  92.7 us
    pallas_call x1, Pallas kernels, on_device(): pl.pallas_call(leave, out_shape=(jax.ShapeDtypeStruct((D, VSH), BF16), ja...  3.34 us

profile of v2, /device:TPU:6, one launch (start us, length us, event | category | flops | bytes accessed | tf_op | source)
XLA Modules:
  0.0 96.6 jit_solution(4551765564852608532)
XLA Ops:
  0.6 92.7 %shard_map.76 = (bf16[8192,384]{1,0:T(8,128)(2,1)S(1)}, f32[8,128]{1,0:T(8,128)S(1)}, bf16[16,1024]{1,0:T(8,128)(2,1)S(1)}) custom-call(bf16[16,8192]{1,0:T(8,128)(2,1)} %hid_ref.1, bf16[8192,384]{1,0:T(8,128)(2,1)} %w_ref.1, s32[4,128]{1,0:T(4,128)} %bitcast.3, s32[4,128]{1,0:T(4,128)} %bitcast.4, f32[2]{0:T(128)} %ref_ref.1), custom_call_target="tpu_custom_call" | custom-call | flops 6442450944 | bytes 6291456 | tf_op jit(solution)/shard_map/pallas_call | solution.py:470
  93.3 3.3 %shard_map.77 = (bf16[8192,384]{1,0:T(8,128)(2,1)}, f32[1]{0:T(128)}, bf16[16,1024]{1,0:T(8,128)(2,1)}) custom-call(bf16[8192,384]{1,0:T(8,128)(2,1)S(1)} %get-tuple-element.9.dw_ref, f32[8,128]{1,0:T(8,128)S(1)} %get-tuple-element.10.loss_ref, bf16[16,1024]{1,0:T(8,128)(2,1)S(1)} %get-tuple-element.11.dh_ref), custom_call_target="tpu_custom_call" | custom-call | tf_op jit(solution)/shard_map/pallas_call | solution.py:516

commit v3 on v2

--- a/solution.py
+++ b/solution.py
@@ -23,7 +23,7 @@
 GA, GB, GQ = 1024, 1536, 384
 SX, SY, SZ = 384, 384, 256
 
-N_SEM = 200
+N_SEM = 53
 
 KC = 1024
 
@@ -57,16 +57,34 @@
     counter = [0]
     sends = []
 
-    def remote(src, dst, **d):
-        i = counter[0]
+    def number():
         counter[0] += 1
+        return counter[0] - 1
+
+    def remote(src, dst, i=None, **d):
+        i_own = number() if i is None else i
         copy = pltpu.make_async_remote_copy(
-            src_ref=src, dst_ref=dst, send_sem=ssem.at[i], recv_sem=rsem.at[i],
+            src_ref=src, dst_ref=dst, send_sem=ssem.at[i_own], recv_sem=rsem.at[i_own],
             device_id=dev(**d), device_id_type=MESH,
         )
         copy.start()
+        if i is None:
+            sends.append(copy)
+            return copy
+
+    def all_of(i, whole, **d):
+        copy = pltpu.make_async_remote_copy(
+            src_ref=whole, dst_ref=whole, send_sem=ssem.at[i], recv_sem=rsem.at[i],
+            device_id=dev(**d), device_id_type=MESH,
+        )
         sends.append(copy)
         return copy
+
+    def fan(pairs, whole):
+        i = number()
+        for src, dst, d in pairs:
+            remote(src, dst, i, **d)
+        return all_of(i, whole, **pairs[0][2])
 
     def rx(copy):
         copy.wait_recv()
@@ -114,58 +132,56 @@
 
     own_a = H.at[y, z, :, pl.ds(col_a, GA)]
     own_qb = H.at[y, z, :, pl.ds(col_q, GQ)]
-    first_a = [remote(own_a, own_a, dy=j) for j in (1, 2, 3)]
-    first_q = [remote(own_qb, own_qb, dy=j) for j in (1, 2, 3)]
+    first_a = fan([(own_a, own_a, dict(dy=j)) for j in (1, 2, 3)], H.at[0:3, z, :, pl.ds(col_a, GA)])
+    first_q = fan([(own_qb, own_qb, dict(dy=j)) for j in (1, 2, 3)], H.at[0:3, z, :, pl.ds(col_q, GQ)])
 
     def both_ways(ref):
         return (remote(ref, ref, dz=1), remote(ref, ref, dz=-1))
 
     def fan_y(zz):
-        return [remote(blk_b(y, zz), blk_b(y, zz), dy=j) for j in (1, 2, 3)]
+        ref = blk_b(y, zz)
+        return fan([(ref, ref, dict(dy=j)) for j in (1, 2, 3)], H.at[0:3, zz, :, pl.ds(col_b, GB)])
 
     def fan_x(zz):
-        return [remote(blk_q(zz), blk_q(zz), dx=j) for j in (1, 2, 3)]
-
-    def hand_over(ref):
-        return remote(ref, ref, dc=1)
+        ref = blk_q(zz)
+        return fan([(ref, ref, dict(dx=j)) for j in (1, 2, 3)], H.at[:, zz, :, pl.ds(col_q0, 3 * GQ)])
 
     handed = {}
     arrivals = {}
 
+    def hand_over(key, ref):
+        if key not in handed:
+            handed[key] = number()
+        remote(ref, ref, handed[key], dc=1)
+
     def hand_on(key, zz):
         from_y, from_x = arrivals.pop(key)
-        for copy in from_y:
-            rx(copy)
-        handed[key].append(hand_over(H.at[:, zz, :, pl.ds(col_b, GB)]))
-        for copy in from_x:
-            rx(copy)
-        handed[key].append(hand_over(H.at[:, zz, :, pl.ds(col_q0, NX * GQ)]))
+        rx(from_y)
+        hand_over(key, H.at[:, zz, :, pl.ds(col_b, GB)])
+        rx(from_x)
+        hand_over(key, H.at[:, zz, :, pl.ds(col_q0, NX * GQ)])
+        handed[key] = all_of(handed[key], H.at[:, zz, :, pl.ds(col_a, HALF)], dc=1)
 
     def logits_of(keys):
         zs = [wrap(z - sign * st, NZ) for st, sign in keys]
         for key in keys:
-            for copy in handed[key]:
-                rx(copy)
-        def step(k, acc):
-            at = pl.ds(pl.multiple_of(k * KC, KC), KC)
-            h = jnp.concatenate([H[yy, zz, :, at] for zz in zs for yy in range(NY)], axis=0)
-            return acc + jnp.dot(h, W[at, :], preferred_element_type=F32)
-
-        acc = lax.fori_loop(0, D // KC, step, jnp.zeros((64 * len(zs), VSH), F32))
+            rx(handed[key])
+        acc = jnp.zeros((64 * len(zs), VSH), F32)
+        for k in range(0, D, KC):
+            h = jnp.concatenate([H[yy, zz, :, k:k + KC] for zz in zs for yy in range(NY)], axis=0)
+            acc = acc + jnp.dot(h, W[k:k + KC, :], preferred_element_type=F32)
         acc = acc.reshape(len(zs), NY, 16, VSH)
         for n, zz in enumerate(zs):
             L[:, zz] = acc[n]
 
     ring_b = both_ways(blk_b(y, z))
     fy = fan_y(z)
-    for copy in first_a:
-        rx(copy)
+    rx(first_a)
     ring_a = both_ways(blk_a(z))
-    for copy in first_q:
-        rx(copy)
+    rx(first_q)
     ring_q = both_ways(blk_q(z))
     fx = fan_x(z)
-    handed[0, 1] = [hand_over(blk_a(z))]
+    hand_over((0, 1), blk_a(z))
     arrivals[0, 1] = (fy, fx)
 
     def halves(yy, zz, col, n, k):
@@ -188,7 +204,7 @@
             rx(ring_a[k])
             ref = blk_a(zz) if s < 3 else halves(slice(None), zz, col_a, GA, k)
             na.append(remote(ref, ref, dz=sign))
-            handed[s, sign] = [hand_over(blk_a(zz))]
+            hand_over((s, sign), blk_a(zz))
             arrivals[s, sign] = (fy, fx)
         for key in list(arrivals):
             if key[0] < s:
@@ -208,7 +224,7 @@
     fx = fan_x(zz)
     rx(ring_a[0])
     rx(ring_a[1])
-    handed[4, -1] = [hand_over(blk_a(zz))]
+    hand_over((4, -1), blk_a(zz))
     arrivals[4, -1] = (fy, fx)
     hand_on((3, 1), wrap(z - 3, NZ))
     hand_on((3, -1), wrap(z + 3, NZ))
@@ -248,14 +264,11 @@
     st = merge(st_own[0], [st_core[...]])
     st_own[1] = st
     group = [(i, j) for i in range(NX) for j in range(NY) if i or j]
-    copies = [remote(st_own.at[1], st_xy.at[n], dx=i, dy=j) for n, (i, j) in enumerate(group)]
-    for copy in copies:
-        rx(copy)
+    rx(fan([(st_own.at[1], st_xy.at[n], dict(dx=i, dy=j)) for n, (i, j) in enumerate(group)], st_xy))
     st = merge(st, [st_xy[n] for n in range(15)])
     st_own[2] = st
-    copies = [remote(st_own.at[2], st_z.at[k - 1], dz=k) for k in range(1, NZ)]
-    for copy in copies:
-        rx(copy)
+    rx(fan([(st_own.at[2], st_z.at[k - 1], dict(dz=k)) for k in range(1, NZ)], st_z))
+    counter[0] = 0
     st = merge(st, [st_z[n] for n in range(7)])
     lse4 = st[0:4, :]
     logp4 = st[4:8, :] - lse4
@@ -282,11 +295,12 @@
         n = 512
 
         def step(i, carry):
-            at = pl.ds(pl.multiple_of(i * n, n), n)
-            h = H[:, :, :, at].reshape(ROWS, n)
-            dw_ref[at, :] = lax.dot_general(
-                h, G[...], (((0,), (0,)), ((), ())), preferred_element_type=F32
-            ).astype(BF16)
+            for k in range(4):
+                at = pl.ds(pl.multiple_of(i * 4 * n + k * n, n), n)
+                h = H[:, :, :, at].reshape(ROWS, n)
+                dw_ref[at, :] = lax.dot_general(
+                    h, G[...], (((0,), (0,)), ((), ())), preferred_element_type=F32
+                ).astype(BF16)
             return carry
 
         lax.fori_loop(first, last, step, 0)
@@ -349,13 +363,21 @@
             remote(s.at[far, hi], h.at[1], **{axis: -1}),
         )
 
-    def send_near(s, h, land, me, n, halves_in, side, axis):
+    def near_parts(side):
+        return (0, lo, hi) if side == 1 else (1, hi, lo)
+
+    def send_near(s, land, me, n, side, axis):
         at = wrap(me + side, n)
-        k = 0 if side == 1 else 1
+        k, _, alone = near_parts(side)
+        return remote(s.at[at, alone], land.at[k, alone], **{axis: side})
+
+    def send_joined(s, h, land, me, n, halves_in, side, axis):
+        at = wrap(me + side, n)
+        k, joined, _ = near_parts(side)
         rx(halves_in[k])
         for i in (0, 1):
             bump(s, (at, 2 * k + i), h[k, i])
-        return remote(s.at[at], land.at[k], **{axis: side})
+        return remote(s.at[at, joined], land.at[k, joined], **{axis: side})
 
     give("x", 2)
     give("y", 2)
@@ -379,19 +401,22 @@
     z4r = remote(sz.at[zat(4), hi], lz4s.at[1], dz=2)
     z1r = remote(sz.at[zat(1)], lz1.at[0], dz=1)
     z1l = remote(sz.at[zat(-1)], lz1.at[1], dz=-1)
+    keep("x", 1)
+    x_in = [send_near(sx, lx1, x, NX, 1, "dx")]
+    keep("x", 3)
+    x_in.append(send_near(sx, lx1, x, NX, -1, "dx"))
     give("y", 1)
     give("y", 3)
+    keep("y", 1)
+    y_in = [send_near(sy, ly1, y, NY, 1, "dy")]
+    keep("y", 3)
+    y_in.append(send_near(sy, ly1, y, NY, -1, "dy"))
     give("x", 0)
     give("y", 0)
-    weight_grad(0, 2)
-    keep("x", 1)
-    xr = send_near(sx, hx, lx1, x, NX, xh, 1, "dx")
-    keep("x", 3)
-    xl = send_near(sx, hx, lx1, x, NX, xh, -1, "dx")
-    keep("y", 1)
-    yr = send_near(sy, hy, ly1, y, NY, yh, 1, "dy")
-    keep("y", 3)
-    yl = send_near(sy, hy, ly1, y, NY, yh, -1, "dy")
+    for side in (1, -1):
+        x_in.append(send_joined(sx, hx, lx1, x, NX, xh, side, "dx"))
+    for side in (1, -1):
+        y_in.append(send_joined(sy, hy, ly1, y, NY, yh, side, "dy"))
     keep("x", 0)
     keep("y", 0)
     rx(z3r)
@@ -404,52 +429,45 @@
     for i in range(NX):
         bump(sz, (zat(2), i), lz3s[0, i], *([lz4s[1, i - 2]] if i >= 2 else []))
     z2r = remote(sz.at[zat(2)], lz2.at[1], dz=2)
-    weight_grad(2, 10)
-
-    rx(xr)
-    rx(xl)
+
+    for copy in x_in:
+        rx(copy)
     for yy in range(NY):
         bump(sx, (x, yy), lx1[0, yy], lx1[1, yy])
-    cx = [remote(sx.at[x, wrap(y + j, NY)], lx2.at[j - 1], dy=j) for j in (1, 2, 3)]
-    rx(yr)
-    rx(yl)
+    cx = fan([(sx.at[x, wrap(y + j, NY)], lx2.at[j - 1], dict(dy=j)) for j in (1, 2, 3)], lx2)
+    for copy in y_in:
+        rx(copy)
     for xx in range(NX):
         bump(sy, (y, xx), ly1[0, xx], ly1[1, xx])
-    cy = [remote(sy.at[y, wrap(x + j, NX)], ly2.at[j - 1], dx=j) for j in (1, 2, 3)]
-    weight_grad(10, 12)
+    cy = fan([(sy.at[y, wrap(x + j, NX)], ly2.at[j - 1], dict(dx=j)) for j in (1, 2, 3)], ly2)
+    weight_grad(0, 2)
     for copy in (z1r, z1l, z2l, z2r):
         rx(copy)
     for xx in range(NX):
         bump(sz, (z, xx), lz1[0, xx], lz1[1, xx], lz2[0, xx], lz2[1, xx])
-    cz = [remote(sz.at[z, wrap(x + j, NX)], lz5.at[j - 1], dx=j) for j in (1, 2, 3)]
-
-    for copy in cx:
-        rx(copy)
+    cz = fan([(sz.at[z, wrap(x + j, NX)], lz5.at[j - 1], dict(dx=j)) for j in (1, 2, 3)], lz5)
+
+    rx(cx)
     bump(sx, (x, y), lx2[0], lx2[1], lx2[2])
-    cx = [remote(sx.at[x, y, zat(k)], lx3.at[k - 1], dz=k) for k in range(1, NZ)]
-    for copy in cy:
-        rx(copy)
+    cx = fan([(sx.at[x, y, zat(k)], lx3.at[k - 1], dict(dz=k)) for k in range(1, NZ)], lx3)
+    rx(cy)
     bump(sy, (y, x), ly2[0], ly2[1], ly2[2])
-    cy = [remote(sy.at[y, x, zat(k)], ly3.at[k - 1], dz=k) for k in range(1, NZ)]
-    for copy in cz:
-        rx(copy)
+    cy = fan([(sy.at[y, x, zat(k)], ly3.at[k - 1], dict(dz=k)) for k in range(1, NZ)], ly3)
+    rx(cz)
     bump(sz, (z, x), lz5[0], lz5[1], lz5[2])
-    cz = [remote(sz.at[z, x, wrap(y + j, NY)], lz3.at[j - 1], dy=j) for j in (1, 2, 3)]
-    weight_grad(12, 16)
-    for copy in cx:
-        rx(copy)
+    cz = fan([(sz.at[z, x, wrap(y + j, NY)], lz3.at[j - 1], dict(dy=j)) for j in (1, 2, 3)], lz3)
+    weight_grad(2, 4)
+    rx(cx)
     total = sx[x, y, z].astype(F32)
     for k in range(7):
         total = total + lx3[k].astype(F32)
     dh_ref[:, 0:SX] = total.astype(BF16)
-    for copy in cy:
-        rx(copy)
+    rx(cy)
     total = sy[y, x, z].astype(F32)
     for k in range(7):
         total = total + ly3[k].astype(F32)
     dh_ref[:, SX:SX + SY] = total.astype(BF16)
-    for copy in cz:
-        rx(copy)
+    rx(cz)
     total = sz[z, x, y].astype(F32)
     for k in range(3):
         total = total + lz3[k].astype(F32)

time: 97.8 us -> 92 us (0.941)
  Pallas kernels: 96 us -> 90.2 us
    pallas_call x1, Pallas kernels: 92.7 us -> 86.8 us  [run_kernel(): pl.pallas_call(fused_kernel, out_shape=(pltpu.VMEM((D, VSH), BF16), pltpu...]
where the time goes in v3:
time: 92 us; the launch traced here: 91 us
  Pallas kernels  90.2 us (98%)
    pallas_call x1, Pallas kernels, run_kernel(): pl.pallas_call(fused_kernel, out_shape=(pltpu.VMEM((D, VSH), BF16), pltpu...  86.8 us
    pallas_call x1, Pallas kernels, on_device(): pl.pallas_call(leave, out_shape=(jax.ShapeDtypeStruct((D, VSH), BF16), ja...  3.34 us

profile of v3, /device:TPU:6, one launch (start us, length us, event | category | flops | bytes accessed | tf_op | source)
XLA Modules:
  0.0 91.0 jit_solution(4662071158881716897)
XLA Ops:
  0.6 86.8 %shard_map.76 = (bf16[8192,384]{1,0:T(8,128)(2,1)S(1)}, f32[8,128]{1,0:T(8,128)S(1)}, bf16[16,1024]{1,0:T(8,128)(2,1)S(1)}) custom-call(bf16[16,8192]{1,0:T(8,128)(2,1)} %hid_ref.1, bf16[8192,384]{1,0:T(8,128)(2,1)} %w_ref.1, s32[4,128]{1,0:T(4,128)} %bitcast.3, s32[4,128]{1,0:T(4,128)} %bitcast.4, f32[2]{0:T(128)} %ref_ref.1), custom_call_target="tpu_custom_call" | custom-call | flops 6442450944 | bytes 6291456 | tf_op jit(solution)/shard_map/pallas_call | solution.py:488
  87.5 3.3 %shard_map.77 = (bf16[8192,384]{1,0:T(8,128)(2,1)}, f32[1]{0:T(128)}, bf16[16,1024]{1,0:T(8,128)(2,1)}) custom-call(bf16[8192,384]{1,0:T(8,128)(2,1)S(1)} %get-tuple-element.9.dw_ref, f32[8,128]{1,0:T(8,128)S(1)} %get-tuple-element.10.loss_ref, bf16[16,1024]{1,0:T(8,128)(2,1)S(1)} %get-tuple-element.11.dh_ref), custom_call_target="tpu_custom_call" | custom-call | tf_op jit(solution)/shard_map/pallas_call | solution.py:534

commit v4 on v3

--- a/solution.py
+++ b/solution.py
@@ -29,13 +29,13 @@
 
 
 def fused_kernel(
-    hid_ref, w_ref, tgt_ref, seq_ref, ref_ref,
+    hid_ref, w_ref, tgt_in, seq_in, ref_in,
     dw_ref, loss_ref, dh_ref,
     H, W, L, logits_t, G,
     st_own, st_core, st_xy, st_z,
     psx, psy, psz, plx, ply, plz, sx, sy, sz,
     hx, lx1, lx2, lx3, hy, ly1, ly2, ly3, lz3s, lz4s, lz1, lz2, lz5, lz3,
-    local_sem, ssem, rsem,
+    tgt_ref, seq_ref, ref_ref, local_sem, ssem, rsem,
 ):
     ctx = lax.axis_index("ctx")
     tp = lax.axis_index("tp")
@@ -47,9 +47,10 @@
     def wrap(v, n):
         return lax.rem(v + n, n)
 
-    def dev(dy=0, dz=0, dx=0, dc=0):
+    def dev(dy=0, dz=0, dx=0, dc=0, to_z=None):
         yy = wrap(y + dy, NY) if dy else y
         zz = wrap(z + dz, NZ) if dz else z
+        zz = zz if to_z is None else to_z
         xx = wrap(x + dx, NX) if dx else x
         cc = 1 - c if dc else c
         return (yy * NZ + zz, xx * 2 + cc)
@@ -111,6 +112,13 @@
     )
     own_q.start()
 
+    small = [
+        pltpu.make_async_copy(src, dst, local_sem.at[3 + n])
+        for n, (src, dst) in enumerate(((tgt_in, tgt_ref), (seq_in, seq_ref), (ref_in, ref_ref)))
+    ]
+    for copy in small:
+        copy.start()
+
     barrier = pltpu.get_barrier_semaphore()
     peers = [dict(dc=1)]
     peers += [dict(dx=i, dy=j) for i in range(NX) for j in range(NY) if i or j]
@@ -118,6 +126,8 @@
     for p in peers:
         pl.semaphore_signal(barrier, inc=1, device_id=dev(**p), device_id_type=MESH)
     pl.semaphore_wait(barrier, len(peers))
+    for copy in small:
+        copy.wait()
     own_ab.wait()
     own_q.wait()
 
@@ -279,7 +289,7 @@
 
     seq0 = total_of(jnp.where(seq4 == 0, logp4, 0.0))
     seq1 = total_of(jnp.where(seq4 == 1, logp4, 0.0))
-    margin = DPO_BETA * ((seq0 - ref_ref[0]) - (seq1 - ref_ref[1]))
+    margin = DPO_BETA * ((seq0 - ref_ref[:, 0:1]) - (seq1 - ref_ref[:, 1:2]))
     neg = jnp.broadcast_to(-margin, (8, 128))
     loss_ref[...] = jnp.maximum(neg, 0.0) + jnp.log1p(jnp.exp(-jnp.abs(neg)))
     pull = (LOSS_SCALE * DPO_BETA) / (1.0 + jnp.exp(margin))
@@ -430,16 +440,36 @@
         bump(sz, (zat(2), i), lz3s[0, i], *([lz4s[1, i - 2]] if i >= 2 else []))
     z2r = remote(sz.at[zat(2)], lz2.at[1], dz=2)
 
+    far, near = (1 - z // 4) * 4, z // 4 * 4
+
+    def second(s, a, b, n, land, axis):
+        return [
+            fan(
+                [
+                    (s.at[a, wrap(b + j, n), pl.ds(h, 4)], land.at[j - 1, pl.ds(h, 4)], {axis: j})
+                    for j in (1, 2, 3)
+                ],
+                land.at[:, pl.ds(h, 4)],
+            )
+            for h in (far, near)
+        ]
+
+    def third(s, a, b, land, out, first):
+        h = far if first else near
+        bump(s, (a, b, pl.ds(h, 4)), *[land[j, pl.ds(h, 4)] for j in range(3)])
+        to = [far + i for i in range(4)] if first else [near + lax.rem(z + k, 4) for k in (1, 2, 3)]
+        return fan([(s.at[a, b, zz], out.at[z], dict(to_z=zz)) for zz in to], out.at[0:len(to)])
+
     for copy in x_in:
         rx(copy)
     for yy in range(NY):
         bump(sx, (x, yy), lx1[0, yy], lx1[1, yy])
-    cx = fan([(sx.at[x, wrap(y + j, NY)], lx2.at[j - 1], dict(dy=j)) for j in (1, 2, 3)], lx2)
+    cx = second(sx, x, y, NY, lx2, "dy")
     for copy in y_in:
         rx(copy)
     for xx in range(NX):
         bump(sy, (y, xx), ly1[0, xx], ly1[1, xx])
-    cy = fan([(sy.at[y, wrap(x + j, NX)], ly2.at[j - 1], dict(dx=j)) for j in (1, 2, 3)], ly2)
+    cy = second(sy, y, x, NX, ly2, "dx")
     weight_grad(0, 2)
     for copy in (z1r, z1l, z2l, z2r):
         rx(copy)
@@ -447,25 +477,29 @@
         bump(sz, (z, xx), lz1[0, xx], lz1[1, xx], lz2[0, xx], lz2[1, xx])
     cz = fan([(sz.at[z, wrap(x + j, NX)], lz5.at[j - 1], dict(dx=j)) for j in (1, 2, 3)], lz5)
 
-    rx(cx)
-    bump(sx, (x, y), lx2[0], lx2[1], lx2[2])
-    cx = fan([(sx.at[x, y, zat(k)], lx3.at[k - 1], dict(dz=k)) for k in range(1, NZ)], lx3)
-    rx(cy)
-    bump(sy, (y, x), ly2[0], ly2[1], ly2[2])
-    cy = fan([(sy.at[y, x, zat(k)], ly3.at[k - 1], dict(dz=k)) for k in range(1, NZ)], ly3)
+    rx(cx[0])
+    cx[0] = third(sx, x, y, lx2, lx3, True)
+    rx(cy[0])
+    cy[0] = third(sy, y, x, ly2, ly3, True)
+    rx(cx[1])
+    cx[1] = third(sx, x, y, lx2, lx3, False)
+    rx(cy[1])
+    cy[1] = third(sy, y, x, ly2, ly3, False)
     rx(cz)
     bump(sz, (z, x), lz5[0], lz5[1], lz5[2])
     cz = fan([(sz.at[z, x, wrap(y + j, NY)], lz3.at[j - 1], dict(dy=j)) for j in (1, 2, 3)], lz3)
     weight_grad(2, 4)
-    rx(cx)
+    rx(cx[0])
+    rx(cx[1])
     total = sx[x, y, z].astype(F32)
-    for k in range(7):
-        total = total + lx3[k].astype(F32)
+    for k in range(1, NZ):
+        total = total + lx3[zat(k)].astype(F32)
     dh_ref[:, 0:SX] = total.astype(BF16)
-    rx(cy)
+    rx(cy[0])
+    rx(cy[1])
     total = sy[y, x, z].astype(F32)
-    for k in range(7):
-        total = total + ly3[k].astype(F32)
+    for k in range(1, NZ):
+        total = total + ly3[zat(k)].astype(F32)
     dh_ref[:, SX:SX + SY] = total.astype(BF16)
     rx(cz)
     total = sz[z, x, y].astype(F32)
@@ -479,7 +513,6 @@
 def run_kernel(hidden, weight, targets, row_seq, ref_logp):
     vmem = pl.BlockSpec(memory_space=pltpu.VMEM)
     hbm = pl.BlockSpec(memory_space=pl.ANY)
-    smem = pl.BlockSpec(memory_space=pltpu.SMEM)
 
     def v16(*shape):
         return pltpu.VMEM(shape, BF16)
@@ -492,7 +525,7 @@
             pltpu.VMEM((8, 128), F32),
             pltpu.VMEM((16, 1024), BF16),
         ),
-        in_specs=[hbm, hbm, vmem, vmem, smem],
+        in_specs=[hbm] * 5,
         out_specs=(vmem, vmem, vmem),
         scratch_shapes=[
             v16(NY, NZ, 16, D),
@@ -505,11 +538,12 @@
             pltpu.VMEM((15, 8, 128), F32),
             pltpu.VMEM((7, 8, 128), F32),
             *chunks, *chunks, *chunks,
-            v16(2, 2, NZ, 16, SX), v16(2, NY, NZ, 16, SX), v16(3, NZ, 16, SX), v16(7, 16, SX),
-            v16(2, 2, NZ, 16, SY), v16(2, NX, NZ, 16, SY), v16(3, NZ, 16, SY), v16(7, 16, SY),
+            v16(2, 2, NZ, 16, SX), v16(2, NY, NZ, 16, SX), v16(3, NZ, 16, SX), v16(NZ, 16, SX),
+            v16(2, 2, NZ, 16, SY), v16(2, NX, NZ, 16, SY), v16(3, NZ, 16, SY), v16(NZ, 16, SY),
             v16(2, NX, NY, 16, SZ), v16(2, 2, NY, 16, SZ), v16(2, NX, NY, 16, SZ),
             v16(2, NX, NY, 16, SZ), v16(3, NY, 16, SZ), v16(3, 16, SZ),
-            pltpu.SemaphoreType.DMA((3,)),
+            pltpu.VMEM((4, 128), jnp.int32), pltpu.VMEM((4, 128), jnp.int32), pltpu.VMEM((1, 2), F32),
+            pltpu.SemaphoreType.DMA((6,)),
             pltpu.SemaphoreType.DMA((N_SEM,)),
             pltpu.SemaphoreType.DMA((N_SEM,)),
         ],
@@ -517,7 +551,7 @@
             collective_id=0, has_side_effects=True, vmem_limit_bytes=52 * 2**20
         ),
         cost_estimate=pl.CostEstimate(flops=2 * 2 * ROWS * D * VSH, bytes_accessed=2 * D * VSH, transcendentals=0),
-    )(hidden, weight, targets.reshape(4, 128), row_seq.reshape(4, 128), ref_logp)
+    )(hidden, weight, targets.reshape(4, 128), row_seq.reshape(4, 128), ref_logp.reshape(1, 2))
 
 
 def on_device(hidden, weight, targets, row_seq, ref_logp):

time: 92 us -> 91.1 us (level)
  no operation moved by 1% of the time
where the time goes in v4:
time: 91.1 us; the launch traced here: 90.2 us
  Pallas kernels  89.4 us (98%)
    pallas_call x1, Pallas kernels, run_kernel(): pl.pallas_call(fused_kernel, out_shape=(pltpu.VMEM((D, VSH), BF16), pltpu...  86.1 us
    pallas_call x1, Pallas kernels, on_device(): pl.pallas_call(leave, out_shape=(jax.ShapeDtypeStruct((D, VSH), BF16), ja...  3.34 us

profile of v4, /device:TPU:6, one launch (start us, length us, event | category | flops | bytes accessed | tf_op | source)
XLA Modules:
  0.0 90.2 jit_solution(9891136788736786532)
XLA Ops:
  0.6 86.1 %shard_map.76 = (bf16[8192,384]{1,0:T(8,128)(2,1)S(1)}, f32[8,128]{1,0:T(8,128)S(1)}, bf16[16,1024]{1,0:T(8,128)(2,1)S(1)}) custom-call(bf16[16,8192]{1,0:T(8,128)(2,1)} %hid_ref.1, bf16[8192,384]{1,0:T(8,128)(2,1)} %w_ref.1, s32[4,128]{1,0:T(4,128)} %bitcast.4, s32[4,128]{1,0:T(4,128)} %bitcast.5, f32[1,2]{1,0:T(1,128)} %bitcast.6), custom_call_target="tpu_custom_call" | custom-call | flops 6442450944 | bytes 6291456 | tf_op jit(solution)/shard_map/pallas_call | solution.py:521
  86.8 3.3 %shard_map.77 = (bf16[8192,384]{1,0:T(8,128)(2,1)}, f32[1]{0:T(128)}, bf16[16,1024]{1,0:T(8,128)(2,1)}) custom-call(bf16[8192,384]{1,0:T(8,128)(2,1)S(1)} %get-tuple-element.9.dw_ref, f32[8,128]{1,0:T(8,128)S(1)} %get-tuple-element.10.loss_ref, bf16[16,1024]{1,0:T(8,128)(2,1)S(1)} %get-tuple-element.11.dh_ref), custom_call_target="tpu_custom_call" | custom-call | tf_op jit(solution)/shard_map/pallas_call | solution.py:568

commit v5 on v4

--- a/solution.py
+++ b/solution.py
@@ -120,9 +120,10 @@
         copy.start()
 
     barrier = pltpu.get_barrier_semaphore()
-    peers = [dict(dc=1)]
-    peers += [dict(dx=i, dy=j) for i in range(NX) for j in range(NY) if i or j]
-    peers += [dict(dz=k) for k in range(1, NZ)]
+    plane = [(i, j) for i in range(NX) for j in range(NY) if i or j]
+    plane.sort(key=lambda p: -min(p[0], NX - p[0]) - min(p[1], NY - p[1]))
+    line = sorted(range(1, NZ), key=lambda k: -min(k, NZ - k))
+    peers = [dict(dx=i, dy=j) for i, j in plane] + [dict(dz=k) for k in line] + [dict(dc=1)]
     for p in peers:
         pl.semaphore_signal(barrier, inc=1, device_id=dev(**p), device_id_type=MESH)
     pl.semaphore_wait(barrier, len(peers))
@@ -242,7 +243,6 @@
     hand_on((4, -1), zz)
     logits_of([(3, 1), (3, -1)])
     logits_of([(0, 1), (4, -1)])
-    drain()
 
     lt = L[...].reshape(ROWS, VSH).T
     logits_t[...] = lt
@@ -273,11 +273,16 @@
     rx(copy)
     st = merge(st_own[0], [st_core[...]])
     st_own[1] = st
-    group = [(i, j) for i in range(NX) for j in range(NY) if i or j]
-    rx(fan([(st_own.at[1], st_xy.at[n], dict(dx=i, dy=j)) for n, (i, j) in enumerate(group)], st_xy))
+    gathered = sends[:]
+    sends.clear()
+    copy = fan([(st_own.at[1], st_xy.at[n], dict(dx=i, dy=j)) for n, (i, j) in enumerate(plane)], st_xy)
+    for earlier in gathered:
+        earlier.wait_send()
+    rx(copy)
     st = merge(st, [st_xy[n] for n in range(15)])
     st_own[2] = st
-    rx(fan([(st_own.at[2], st_z.at[k - 1], dict(dz=k)) for k in range(1, NZ)], st_z))
+    rx(fan([(st_own.at[2], st_z.at[n], dict(dz=k)) for n, k in enumerate(line)], st_z))
+    drain()
     counter[0] = 0
     st = merge(st, [st_z[n] for n in range(7)])
     lse4 = st[0:4, :]
@@ -489,6 +494,7 @@
     bump(sz, (z, x), lz5[0], lz5[1], lz5[2])
     cz = fan([(sz.at[z, x, wrap(y + j, NY)], lz3.at[j - 1], dict(dy=j)) for j in (1, 2, 3)], lz3)
     weight_grad(2, 4)
+    drain()
     rx(cx[0])
     rx(cx[1])
     total = sx[x, y, z].astype(F32)
@@ -506,8 +512,6 @@
     for k in range(3):
         total = total + lz3[k].astype(F32)
     dh_ref[:, SX + SY:] = total.astype(BF16)
-
-    drain()
 
 
 def run_kernel(hidden, weight, targets, row_seq, ref_logp):

time: 91.1 us -> 90.7 us (level)
  no operation moved by 1% of the time
where the time goes in v5:
time: 90.7 us; the launch traced here: 90.2 us
  Pallas kernels  89.4 us (99%)
    pallas_call x1, Pallas kernels, run_kernel(): pl.pallas_call(fused_kernel, out_shape=(pltpu.VMEM((D, VSH), BF16), pltpu...  86 us
    pallas_call x1, Pallas kernels, on_device(): pl.pallas_call(leave, out_shape=(jax.ShapeDtypeStruct((D, VSH), BF16), ja...  3.34 us

profile of v5, /device:TPU:6, one launch (start us, length us, event | category | flops | bytes accessed | tf_op | source)
XLA Modules:
  0.0 90.2 jit_solution(13180615139581876471)
XLA Ops:
  0.6 86.0 %shard_map.76 = (bf16[8192,384]{1,0:T(8,128)(2,1)S(1)}, f32[8,128]{1,0:T(8,128)S(1)}, bf16[16,1024]{1,0:T(8,128)(2,1)S(1)}) custom-call(bf16[16,8192]{1,0:T(8,128)(2,1)} %hid_ref.1, bf16[8192,384]{1,0:T(8,128)(2,1)} %w_ref.1, s32[4,128]{1,0:T(4,128)} %bitcast.4, s32[4,128]{1,0:T(4,128)} %bitcast.5, f32[1,2]{1,0:T(1,128)} %bitcast.6), custom_call_target="tpu_custom_call" | custom-call | flops 6442450944 | bytes 6291456 | tf_op jit(solution)/shard_map/pallas_call | solution.py:525
  86.7 3.3 %shard_map.77 = (bf16[8192,384]{1,0:T(8,128)(2,1)}, f32[1]{0:T(128)}, bf16[16,1024]{1,0:T(8,128)(2,1)}) custom-call(bf16[8192,384]{1,0:T(8,128)(2,1)S(1)} %get-tuple-element.9.dw_ref, f32[8,128]{1,0:T(8,128)S(1)} %get-tuple-element.10.loss_ref, bf16[16,1024]{1,0:T(8,128)(2,1)S(1)} %get-tuple-element.11.dh_ref), custom_call_target="tpu_custom_call" | custom-call | tf_op jit(solution)/shard_map/pallas_call | solution.py:572

commit v6 on v5

--- a/solution.py
+++ b/solution.py
@@ -396,14 +396,14 @@
 
     give("x", 2)
     give("y", 2)
+    give("x", 1)
+    give("x", 3)
     for j in range(4):
         give("z", j)
     keep("x", 2)
     xh = send_halves(sx, hx, x, NX, dx=0)
     keep("y", 2)
     yh = send_halves(sy, hy, y, NY, dy=0)
-    give("x", 1)
-    give("x", 3)
     for j in range(4):
         keep("z", j)
 

time: 90.7 us -> 90.5 us (level)
  no operation moved by 1% of the time
where the time goes in v6:
time: 90.5 us; the launch traced here: 90.1 us
  Pallas kernels  89.3 us (99%)
    pallas_call x1, Pallas kernels, run_kernel(): pl.pallas_call(fused_kernel, out_shape=(pltpu.VMEM((D, VSH), BF16), pltpu...  86 us
    pallas_call x1, Pallas kernels, on_device(): pl.pallas_call(leave, out_shape=(jax.ShapeDtypeStruct((D, VSH), BF16), ja...  3.34 us

profile of v6, /device:TPU:6, one launch (start us, length us, event | category | flops | bytes accessed | tf_op | source)
XLA Modules:
  0.0 90.1 jit_solution(13001391490564781587)
XLA Ops:
  0.6 86.0 %shard_map.76 = (bf16[8192,384]{1,0:T(8,128)(2,1)S(1)}, f32[8,128]{1,0:T(8,128)S(1)}, bf16[16,1024]{1,0:T(8,128)(2,1)S(1)}) custom-call(bf16[16,8192]{1,0:T(8,128)(2,1)} %hid_ref.1, bf16[8192,384]{1,0:T(8,128)(2,1)} %w_ref.1, s32[4,128]{1,0:T(4,128)} %bitcast.4, s32[4,128]{1,0:T(4,128)} %bitcast.5, f32[1,2]{1,0:T(1,128)} %bitcast.6), custom_call_target="tpu_custom_call" | custom-call | flops 6442450944 | bytes 6291456 | tf_op jit(solution)/shard_map/pallas_call | solution.py:525
  86.6 3.3 %shard_map.77 = (bf16[8192,384]{1,0:T(8,128)(2,1)}, f32[1]{0:T(128)}, bf16[16,1024]{1,0:T(8,128)(2,1)}) custom-call(bf16[8192,384]{1,0:T(8,128)(2,1)S(1)} %get-tuple-element.9.dw_ref, f32[8,128]{1,0:T(8,128)S(1)} %get-tuple-element.10.loss_ref, bf16[16,1024]{1,0:T(8,128)(2,1)S(1)} %get-tuple-element.11.dh_ref), custom_call_target="tpu_custom_call" | custom-call | tf_op jit(solution)/shard_map/pallas_call | solution.py:572
